TPU v7x, 32 devices: a whole 2x2x4 slice. The times are simulated.
32 devices in a mesh: dp: 4 (over z), seq: 8 (over y, x, core).
Axes of the slice: x: 2, y: 2, z: 4, core: 2. Of those that a mesh axis runs over, the one named last changes fastest.
Arguments:
- tokens: bfloat16 [4, 8192, 768], P('dp', 'seq'), may hold values from -6 to 6
- cotangent: bfloat16 [4, 8192, 768], P('dp', 'seq'), may hold values from -6 to 6
- first_gain: float32 [768], replicated, may hold values from 0.25 to 1.75
- first_shift: float32 [768], replicated, may hold values from -1.75 to 1.75
- joint_weight: bfloat16 [768, 2304], replicated, may hold values from -0.21875 to 0.21875
- query_bias: float32 [768], replicated, may hold values from -3 to 3
- value_bias: float32 [768], replicated, may hold values from -3 to 3
- score_weight: bfloat16 [768, 12], replicated, may hold values from -0.3125 to 0.3125
- out_weight: bfloat16 [768, 768], replicated, may hold values from -1.75 to 1.75
- out_bias: float32 [768], replicated, may hold values from -3 to 3
- second_gain: float32 [768], replicated, may hold values from 0.25 to 1.75
- second_shift: float32 [768], replicated, may hold values from -1.75 to 1.75
- expand_weight: bfloat16 [768, 3072], replicated, may hold values from -0.21875 to 0.21875
- expand_bias: float32 [3072], replicated, may hold values from -3 to 3
- reduce_weight: bfloat16 [3072, 768], replicated, may hold values from -0.109375 to 0.109375
- reduce_bias: float32 [768], replicated, may hold values from -3 to 3
- picks: int32 [4, 8, 8, 8], P('dp', 'seq'), may hold values from 0 to 1023
- quota: int32 [4, 8, 8], P('dp', 'seq'), may hold values from 0 to 8, as said below
Outputs:
- layer_out: bfloat16 [4, 8192, 768], P('dp', 'seq')
- token_grad: float32 [4, 8192, 768], P('dp', 'seq')
- first_gain_grad: float32 [768], replicated
- first_shift_grad: float32 [768], replicated
- joint_weight_grad: float32 [768, 2304], replicated
- query_bias_grad: float32 [768], replicated
- value_bias_grad: float32 [768], replicated
- score_weight_grad: float32 [768, 12], replicated
- out_weight_grad: float32 [768, 768], replicated
- out_bias_grad: float32 [768], replicated
- second_gain_grad: float32 [768], replicated
- second_shift_grad: float32 [768], replicated
- expand_weight_grad: float32 [768, 3072], replicated
- expand_bias_grad: float32 [3072], replicated
- reduce_weight_grad: float32 [3072, 768], replicated
- reduce_bias_grad: float32 [768], replicated
Inputs may be any that keep to these rules, and one draw needn't show every extreme that they name: quota[s, d] is zero where s > d; the last query block takes 8 keys from every block. `picks`: only entries with c < quota[s, d] are read.
All inputs are finite; a program needn't handle non-finite values.
Results may differ from a plain program's by a relative error of at most 0.011.
Values may be sent and summed in bfloat16 or wider, within the bound.
No kernel may reach another device: no remote copies, remote signals or barrier semaphores. Data moves between devices by JAX's collectives and lax.ppermute only.
A program may use at most 192 MiB of HBM per device.

v0:
```python
import math
import jax
import jax.numpy as jnp
from jax import lax
from jax.sharding import PartitionSpec as P

WIN = 64
PICK = 8
epsilon = 1e-05
very_low = -1e30


def passed_along(value, axis, steps):
    count = lax.axis_size(axis)
    leading, last = (max(0, -steps), min(count, count - steps))
    return lax.ppermute(value, axis, [(source, source + steps) for source in range(leading, last)])


def layer_norm_parts(values, gain, shift):
    average = jnp.mean(values, axis=-1, keepdims=True)
    centred = values - average
    variance = jnp.mean(centred * centred, axis=-1, keepdims=True)
    inverse = lax.rsqrt(variance + epsilon)
    unit = centred * inverse
    return (unit * gain + shift, unit, inverse)


def layer_norm_back(grad_out, unit, inverse, gain):
    grad_unit = grad_out * gain
    mean_grad = jnp.mean(grad_unit, axis=-1, keepdims=True)
    mean_cross = jnp.mean(grad_unit * unit, axis=-1, keepdims=True)
    grad_in = (grad_unit - mean_grad - unit * mean_cross) * inverse
    return (grad_in, jnp.sum(grad_out * unit, axis=0), jnp.sum(grad_out, axis=0))


def gelu_tanh(values):
    return (
        0.5
        * values
        * (1.0 + jnp.tanh(0.7978845608028654 * (values + 0.044715 * values * values * values)))
    )


def cross(left, right):
    return lax.dot_general(
        left, right, (((0,), (0,)), ((), ())), preferred_element_type=jnp.float32
    )


def times_transposed(left, right):
    return lax.dot_general(
        left, right, (((1,), (1,)), ((), ())), preferred_element_type=jnp.float32
    )


def pair_tiles(values, tiles, window):
    shaped = values.reshape((tiles + 1, window) + values.shape[1:])
    return jnp.concatenate([shaped[:-1], shaped[1:]], axis=1)


def arrange(rim, packed, far_packed, far_pos, place, heads, head_size):
    rows = packed.shape[0]
    width = heads * head_size
    tiles = rows // WIN
    near = pair_tiles(jnp.concatenate([rim, packed], axis=0), tiles, WIN)
    near_key = near[..., :width].reshape(tiles, 2 * WIN, heads, head_size)
    near_value = near[..., width : 2 * width].reshape(tiles, 2 * WIN, heads, head_size)
    near_score = near[..., 2 * width :].astype(jnp.float32)
    far_flat = far_packed.reshape(-1, far_packed.shape[-1])
    far_key = far_flat[:, :width].reshape(-1, heads, head_size)
    far_value = far_flat[:, width : 2 * width].reshape(-1, heads, head_size)
    far_score = far_flat[:, 2 * width :].astype(jnp.float32)
    start = place * rows
    ext_pos = start - WIN + jnp.arange(rows + WIN, dtype=jnp.int32)
    near_pos = pair_tiles(ext_pos, tiles, WIN)
    query_pos = (start + jnp.arange(rows, dtype=jnp.int32)).reshape(tiles, WIN)
    near_mask = (
        (near_pos[:, None, :] <= query_pos[:, :, None])
        & (near_pos[:, None, :] > query_pos[:, :, None] - WIN)
        & (near_pos[:, None, :] >= 0)
    )[:, None]
    far_mask = (far_pos.reshape(-1)[None, None, :] <= query_pos[:, :, None] - WIN)[:, None]
    return (near_key, near_value, near_score, far_key, far_value, far_score, near_mask, far_mask)


def attention_logits(query_tiles, keys_set, scale):
    near_key, near_value, near_score, far_key, far_value, far_score, near_mask, far_mask = keys_set
    near_raw = jnp.einsum(
        "tqhd,tkhd->thqk", query_tiles, near_key, preferred_element_type=jnp.float32
    )
    far_raw = jnp.einsum("tqhd,khd->thqk", query_tiles, far_key, preferred_element_type=jnp.float32)
    near_gate = jnp.transpose(jax.nn.log_sigmoid(near_score), (0, 2, 1))[:, :, None, :]
    far_gate = jnp.transpose(jax.nn.log_sigmoid(far_score))[None, :, None, :]
    near_logit = jnp.where(near_mask, near_raw * scale + near_gate, very_low)
    far_logit = jnp.where(far_mask, far_raw * scale + far_gate, very_low)
    return (near_logit, far_logit)


def attention_back(query_tiles, keys_set, grad_mixed, log_total, scale):
    near_key, near_value, near_score, far_key, far_value, far_score, near_mask, far_mask = keys_set
    near_logit, far_logit = attention_logits(query_tiles, keys_set, scale)
    near_prob = jnp.exp(near_logit - log_total[..., None])
    far_prob = jnp.exp(far_logit - log_total[..., None])
    near_low = near_prob.astype(jnp.bfloat16)
    far_low = far_prob.astype(jnp.bfloat16)
    grad_near_prob = jnp.einsum(
        "tqhd,tkhd->thqk", grad_mixed, near_value, preferred_element_type=jnp.float32
    )
    grad_far_prob = jnp.einsum(
        "tqhd,khd->thqk", grad_mixed, far_value, preferred_element_type=jnp.float32
    )
    delta = jnp.sum(near_prob * grad_near_prob, axis=-1) + jnp.sum(
        far_prob * grad_far_prob, axis=-1
    )
    grad_near_logit = near_prob * (grad_near_prob - delta[..., None])
    grad_far_logit = far_prob * (grad_far_prob - delta[..., None])
    near_raw_low = (grad_near_logit * scale).astype(jnp.bfloat16)
    far_raw_low = (grad_far_logit * scale).astype(jnp.bfloat16)
    grad_query = jnp.einsum(
        "thqk,tkhd->tqhd", near_raw_low, near_key, preferred_element_type=jnp.float32
    )
    grad_query = grad_query + jnp.einsum(
        "thqk,khd->tqhd", far_raw_low, far_key, preferred_element_type=jnp.float32
    )
    grad_near_key = jnp.einsum(
        "thqk,tqhd->tkhd", near_raw_low, query_tiles, preferred_element_type=jnp.float32
    )
    grad_near_value = jnp.einsum(
        "thqk,tqhd->tkhd", near_low, grad_mixed, preferred_element_type=jnp.float32
    )
    grad_near_score = jnp.transpose(jnp.sum(grad_near_logit, axis=2), (0, 2, 1)) * jax.nn.sigmoid(
        -near_score
    )
    grad_far_key = jnp.einsum(
        "thqk,tqhd->khd", far_raw_low, query_tiles, preferred_element_type=jnp.float32
    )
    grad_far_value = jnp.einsum(
        "thqk,tqhd->khd", far_low, grad_mixed, preferred_element_type=jnp.float32
    )
    grad_far_score = jnp.transpose(jnp.sum(grad_far_logit, axis=(0, 2))) * jax.nn.sigmoid(
        -far_score
    )
    tiles = grad_near_key.shape[0]
    span = grad_near_key.shape[1]
    near_pack = jnp.concatenate(
        [
            grad_near_key.reshape(tiles, span, -1),
            grad_near_value.reshape(tiles, span, -1),
            grad_near_score,
        ],
        axis=-1,
    )
    slots = grad_far_key.shape[0]
    far_pack = jnp.concatenate(
        [grad_far_key.reshape(slots, -1), grad_far_value.reshape(slots, -1), grad_far_score],
        axis=-1,
    )
    return (grad_query, near_pack, far_pack)


def per_device(
    tokens,
    cotangent,
    first_gain,
    first_shift,
    joint_weight,
    query_bias,
    value_bias,
    score_weight,
    out_weight,
    out_bias,
    second_gain,
    second_shift,
    expand_weight,
    expand_bias,
    reduce_weight,
    reduce_bias,
    picks,
    quota,
):
    rows = tokens.shape[1]
    width = tokens.shape[2]
    heads = score_weight.shape[1]
    head_size = width // heads
    tiles = rows // WIN
    blocks = lax.axis_size("seq")
    place = lax.axis_index("seq")
    scale = 1.0 / math.sqrt(head_size)
    inputs = tokens[0].astype(jnp.float32)
    normed, unit_one, inverse_one = layer_norm_parts(inputs, first_gain, first_shift)
    normed_low = normed.astype(jnp.bfloat16)
    joint = jnp.dot(normed_low, joint_weight, preferred_element_type=jnp.float32)
    query = (joint[:, :width] + query_bias).astype(jnp.bfloat16)
    keys = joint[:, width : 2 * width].astype(jnp.bfloat16)
    values = (joint[:, 2 * width :] + value_bias).astype(jnp.bfloat16)
    score = jnp.dot(normed_low, score_weight, preferred_element_type=jnp.float32).astype(
        jnp.bfloat16
    )
    packed = jnp.concatenate([keys, values, score], axis=1)
    channels = packed.shape[1]
    pick_rows = picks[0, 0]
    flat_rows = pick_rows.reshape(-1)
    live = jnp.arange(PICK, dtype=jnp.int32)[None, :] < quota[0, 0][:, None]
    positions = jnp.where(live, place * rows + pick_rows, 2 * rows * blocks)
    sent = packed[flat_rows].reshape(blocks, PICK, channels)
    rim = passed_along(packed[rows - WIN :], "seq", 1)
    far_packed, far_pos = (
        lax.all_to_all(sent, "seq", split_axis=0, concat_axis=0, tiled=True),
        lax.all_to_all(positions, "seq", split_axis=0, concat_axis=0, tiled=True),
    )
    keys_set = arrange(rim, packed, far_packed, far_pos, place, heads, head_size)
    query_tiles = query.reshape(tiles, WIN, heads, head_size)
    near_logit, far_logit = attention_logits(query_tiles, keys_set, scale)
    top = jnp.maximum(jnp.max(near_logit, axis=-1), jnp.max(far_logit, axis=-1))
    total = jnp.sum(jnp.exp(near_logit - top[..., None]), axis=-1) + jnp.sum(
        jnp.exp(far_logit - top[..., None]), axis=-1
    )
    log_total = top + jnp.log(total)
    near_low = jnp.exp(near_logit - log_total[..., None]).astype(jnp.bfloat16)
    far_low = jnp.exp(far_logit - log_total[..., None]).astype(jnp.bfloat16)
    mixed = jnp.einsum("thqk,tkhd->tqhd", near_low, keys_set[1], preferred_element_type=jnp.float32)
    mixed = mixed + jnp.einsum(
        "thqk,khd->tqhd", far_low, keys_set[4], preferred_element_type=jnp.float32
    )
    mixed_low = mixed.reshape(rows, width).astype(jnp.bfloat16)
    attn = jnp.dot(mixed_low, out_weight, preferred_element_type=jnp.float32) + out_bias
    resid = inputs + attn
    normed_two, unit_two, inverse_two = layer_norm_parts(resid, second_gain, second_shift)
    normed_two_low = normed_two.astype(jnp.bfloat16)
    pre = jnp.dot(normed_two_low, expand_weight, preferred_element_type=jnp.float32) + expand_bias
    activated, gelu_pull = jax.vjp(gelu_tanh, pre)
    hidden_low = activated.astype(jnp.bfloat16)
    layer_out = (
        resid + jnp.dot(hidden_low, reduce_weight, preferred_element_type=jnp.float32) + reduce_bias
    ).astype(jnp.bfloat16)
    grad_out_low = cotangent[0]
    grad_out = grad_out_low.astype(jnp.float32)
    reduce_bias_grad = jnp.sum(grad_out, axis=0)
    grad_hidden = times_transposed(grad_out_low, reduce_weight)
    grad_pre_low = gelu_pull(grad_hidden)[0].astype(jnp.bfloat16)
    expand_bias_grad = jnp.sum(grad_pre_low.astype(jnp.float32), axis=0)
    grad_normed_two = times_transposed(grad_pre_low, expand_weight)
    grad_resid_norm, second_gain_grad, second_shift_grad = layer_norm_back(
        grad_normed_two, unit_two, inverse_two, second_gain
    )
    grad_resid = grad_out + grad_resid_norm
    grad_attn_low = grad_resid.astype(jnp.bfloat16)
    out_bias_grad = jnp.sum(grad_attn_low.astype(jnp.float32), axis=0)
    grad_mixed_low = (
        times_transposed(grad_attn_low, out_weight)
        .astype(jnp.bfloat16)
        .reshape(tiles, WIN, heads, head_size)
    )
    rim_back_set = passed_along(packed[rows - WIN :], "seq", 1)
    far_again, pos_again = (
        lax.all_to_all(sent, "seq", split_axis=0, concat_axis=0, tiled=True),
        lax.all_to_all(positions, "seq", split_axis=0, concat_axis=0, tiled=True),
    )
    keys_back = arrange(rim_back_set, packed, far_again, pos_again, place, heads, head_size)
    grad_query, near_pack, far_pack = attention_back(
        query_tiles, keys_back, grad_mixed_low, log_total, scale
    )
    grad_query_low = grad_query.reshape(rows, width).astype(jnp.bfloat16)
    zero_tile = jnp.zeros((1, WIN, channels), jnp.float32)
    extended = jnp.concatenate([near_pack[:, :WIN], zero_tile], axis=0) + jnp.concatenate(
        [zero_tile, near_pack[:, WIN:]], axis=0
    )
    rim_grad = extended[0]
    own_grad = extended[1:].reshape(rows, channels)
    far_grad_low = far_pack.astype(jnp.bfloat16).reshape(blocks, PICK, channels)
    back_far = lax.all_to_all(far_grad_low, "seq", split_axis=0, concat_axis=0, tiled=True)
    back_rim = passed_along(rim_grad.astype(jnp.bfloat16), "seq", -1)
    own_total = own_grad + jnp.concatenate(
        [jnp.zeros((rows - WIN, channels), jnp.float32), back_rim.astype(jnp.float32)], axis=0
    )
    own_total = own_total.at[flat_rows].add(
        back_far.reshape(blocks * PICK, channels).astype(jnp.float32)
    )
    grad_packed_low = own_total.astype(jnp.bfloat16)
    grad_key_low = grad_packed_low[:, :width]
    grad_value_low = grad_packed_low[:, width : 2 * width]
    grad_score_low = grad_packed_low[:, 2 * width :]
    grad_joint_low = jnp.concatenate([grad_query_low, grad_key_low, grad_value_low], axis=1)
    query_bias_grad = jnp.sum(grad_query_low.astype(jnp.float32), axis=0)
    value_bias_grad = jnp.sum(grad_value_low.astype(jnp.float32), axis=0)
    score_weight_grad = cross(normed_low, grad_score_low)
    grad_normed = times_transposed(grad_joint_low, joint_weight) + times_transposed(
        grad_score_low, score_weight
    )
    grad_input_norm, first_gain_grad, first_shift_grad = layer_norm_back(
        grad_normed, unit_one, inverse_one, first_gain
    )
    token_grad = (grad_resid + grad_input_norm)[None]
    joint_weight_grad = cross(normed_low, grad_joint_low)
    out_weight_grad = cross(mixed_low, grad_attn_low)
    expand_weight_grad = cross(normed_two_low, grad_pre_low)
    reduce_weight_grad = cross(hidden_low, grad_out_low)
    (
        first_gain_grad,
        first_shift_grad,
        joint_weight_grad,
        query_bias_grad,
        value_bias_grad,
        score_weight_grad,
        out_weight_grad,
        out_bias_grad,
        second_gain_grad,
        second_shift_grad,
        expand_weight_grad,
        expand_bias_grad,
        reduce_weight_grad,
        reduce_bias_grad,
    ) = lax.psum(
        (
            first_gain_grad,
            first_shift_grad,
            joint_weight_grad,
            query_bias_grad,
            value_bias_grad,
            score_weight_grad,
            out_weight_grad,
            out_bias_grad,
            second_gain_grad,
            second_shift_grad,
            expand_weight_grad,
            expand_bias_grad,
            reduce_weight_grad,
            reduce_bias_grad,
        ),
        ("dp", "seq"),
    )
    return (
        layer_out[None],
        token_grad,
        first_gain_grad,
        first_shift_grad,
        joint_weight_grad,
        query_bias_grad,
        value_bias_grad,
        score_weight_grad,
        out_weight_grad,
        out_bias_grad,
        second_gain_grad,
        second_shift_grad,
        expand_weight_grad,
        expand_bias_grad,
        reduce_weight_grad,
        reduce_bias_grad,
    )


def solution(mesh):
    placed = (
        P("dp", "seq", None),
        P("dp", "seq", None),
        P(),
        P(),
        P(),
        P(),
        P(),
        P(),
        P(),
        P(),
        P(),
        P(),
        P(),
        P(),
        P(),
        P(),
        P("dp", "seq", None, None),
        P("dp", "seq", None),
    )
    return jax.shard_map(
        per_device,
        mesh=mesh,
        in_specs=placed,
        out_specs=(
            P("dp", "seq", None),
            P("dp", "seq", None),
            P(),
            P(),
            P(),
            P(),
            P(),
            P(),
            P(),
            P(),
            P(),
            P(),
            P(),
            P(),
            P(),
            P(),
        ),
        check_vma=False,
    )
```

profile of v0, /device:TPU:0, one launch (start us, length us, event | category | flops | bytes accessed | tf_op | source)
XLA Modules:
  0.0 999.5 jit_solution(8566734394154111945)
XLA Ops:
  24.6 5.4 fusion.151
  58.0 9.3 copy.263
  83.5 7.7 fusion.147
  92.9 5.6 pad_maximum_fusion.2
  98.5 9.3 copy.262
  116.2 6.9 fusion.148
  152.4 8.4 fusion.143
  160.8 10.7 %fusion.73 = f32[3072,768]{1,0:T(8,128)} fusion(bf16[1,1024,768]{2,1,0:T(8,128)(2,1)S(1)} %copy-done.30, f32[1024,3072]{1,0:T(8,128)S(1)} %fusion.143, f32[3072]{0:T(1024)S(1)} %copy-done.62), kind=kOutput, calls=%fused_computation.117 | convolution fusion | flops 4863295488 | bytes 23605248 | tf_op jit(solution)/shard_map/dot_general | solution.py:45
  171.6 18.3 %convert_reduce_fusion = (f32[3072]{0:T(1024)}, bf16[1024,3072]{1,0:T(8,128)(2,1)}) fusion(bf16[3072,768]{1,0:T(8,128)(2,1)} %param.32, bf16[1,1024,768]{2,1,0:T(8,128)(2,1)} %param.19, f32[1024,3072]{1,0:T(8,128)S(1)} %fusion.143, f32[3072]{0:T(1024)S(1)} %copy-done.62), kind=kOutput, calls=%fused_computation.13 | convolution fusion | flops 4916769792 | bytes 25190400 | tf_op jit(solution)/shard_map/dot_general | solution.py:51
  189.9 10.5 %fusion.150 = (f32[768]{0:T(1024)}, f32[1024,768]{1,0:T(8,128)}) fusion(bf16[1024,3072]{1,0:T(8,128)(2,1)} %get-tuple-element.170, bf16[768,3072]{1,0:T(8,128)(2,1)} %param.30), kind=kOutput, calls=%fused_computation.212 | convolution fusion | flops 4832623616 | bytes 14158848 | tf_op jit(solution)/shard_map/dot_general | solution.py:51
  200.3 7.9 fusion.142
  233.8 5.8 fusion.94
  239.6 9.2 multiply_reduce_fusion
  264.5 6.5 copy.298
  271.0 9.7 multiply_convert_fusion.2
  283.7 7.4 fusion.54
  291.1 6.5 copy.297
  297.6 9.9 pad_maximum_fusion
  307.5 11.4 %fusion.144 = (f32[16,64,1548]{2,1,0:T(8,128)}, f32[16,64,1548]{2,1,0:T(8,128)}) fusion(f32[16,128,1548]{2,1,0:T(8,128)} %pad_maximum_fusion), kind=kLoop, calls=%fused_computation.206 | loop fusion | bytes 25362432 | tf_op jit(solution)/shard_map/slice | solution.py:266
  343.4 8.6 convert_reduce_fusion.1
  352.6 6.5 copy.330
  359.1 6.1 reshape.331
  365.1 6.2 bitcast_add_fusion
  371.3 7.4 scatter_custom_fusion
  386.6 6.9 fusion.28
  393.6 9.6 fusion.38
  403.2 12.0 %fusion.78 = bf16[1,1024,768]{1,2,0:T(8,128)(2,1)} fusion(f32[768]{0:T(1024)} %param.33, f32[1024,768]{0,1:T(8,128)} %copy-done.6, bf16[3072,768]{1,0:T(8,128)(2,1)} %param.32, f32[1024,3072]{1,0:T(8,128)} %copy-done.18, f32[3072]{0:T(1024)} %param.31), kind=kOutput, calls=%fused_computation.122 | convolution fusion | flops 4865654784 | bytes 22035456 | tf_op jit(solution)/shard_map/dot_general | solution.py:234
  418.5 5.9 fusion.27
  428.0 94.7 %all-reduce.8.cloned.1.call-done = (f32[768]{0:T(1024)}, f32[768]{0:T(1024)}, f32[768]{0:T(1024)}, f32[768]{0:T(1024)}, f32[768,12]{0,1:T(8,128)}, /*index=5*/f3...) async-done(((f32[768]{0:T(1024)}, f32[768]{0:T(1024)}, f32[768]{0:T(1024)}, f32[768]{0:T(1024)}, f32[768,12]{0,1:T(8,128)}, ...) | async-done | bytes 73744 | tf_op jit(solution)/shard_map/psum | solution.py:313
  522.7 441.9 %all-reduce.10.cloned.1.call-done = (f32[768,2304]{1,0:T(8,128)}, f32[768,768]{1,0:T(8,128)}, f32[768,3072]{1,0:T(8,128)}, f32[3072,768]{1,0:T(8,128)}) async-done(((f32[768,2304]{1,0:T(8,128)}, f32[768,768]{1,0:T(8,128)}, f32[768,3072]{1,0:T(8,128)}, f32[3072,768]{1,0:T(8,128)}), (f32[768,2304]{1,0:T(8,128)}, f32[768,768]{1,0:T(8,128)}, f32[768,3072]{1,0:T(8,128)}, ...) | async-done | bytes 28311568 | tf_op jit(solution)/shard_map/psum | solution.py:313
  967.1 6.6 copy.431
  978.7 8.8 copy.439
  (267 shorter events, 196.9 us)
Async XLA Ops:
  7.2 17.4 %copy-start = (bf16[768,2304]{1,0:T(8,128)(2,1)S(1)}, bf16[768,2304]{1,0:T(8,128)(2,1)}, u32[]{:S(2)}) copy-start(bf16[768,2304]{1,0:T(8,128)(2,1)} %param.22) | copy-start | bytes 10616836
  7.2 13.0 %copy-start.47 = (f32[768]{0:T(1024)S(1)}, f32[768]{0:T(1024)}, u32[]{:S(2)}) copy-start(f32[768]{0:T(1024)} %param.20) | copy-start | bytes 9220
  7.2 13.0 %copy-start.51 = (f32[768]{0:T(1024)S(1)}, f32[768]{0:T(1024)}, u32[]{:S(2)}) copy-start(f32[768]{0:T(1024)} %param.21) | copy-start | bytes 9220
  8.7 58.6 %all-to-all-start = ((s32[8,1,8]{2,1,0:T(1,128)}), s32[8,1,8]{2,1,0:T(1,128)}, u32[]{:S(2)}, u32[]{:S(2)}) async-start(s32[8,1,8]{2,1,0:T(1,128)} %bitcast.8), calls=%async_computation | async-start | bytes 8192 | tf_op jit(solution)/shard_map/all_to_all | solution.py:209
  35.6 57.3 %collective-permute-start = (bf16[64,1548]{1,0:T(8,128)(2,1)}, bf16[64,1548]{1,0:T(8,128)(2,1)}, u32[]{:S(2)}, u32[]{:S(2)}) collective-permute-start(bf16[64,1548]{1,0:T(8,128)(2,1)} %slice.111), channel_id=1, source_target_pairs={{0,1},{1,2},{2,3},{3,4},{4,5},{5,6},{6,7},{8,9},{9,10},{10,11},{11... | collective-permute-start | bytes 594440 | tf_op jit(solution)/shard_map/ppermute | solution.py:16
  67.3 10.6 %all-to-all-start.1 = ((bf16[8,8,1548]{2,1,0:T(8,128)(2,1)}), bf16[8,8,1548]{2,1,0:T(8,128)(2,1)}, u32[]{:S(2)}, u32[]{:S(2)}) async-start(bf16[8,8,1548]{2,1,0:T(8,128)(2,1)} %bitcast.194), calls=%async_computation.1 | async-start | bytes 425984 | tf_op jit(solution)/shard_map/all_to_all | solution.py:208
  116.1 16.9 %copy-start.10 = (bf16[16,128,768]{1,0,2:T(8,128)(2,1)}, bf16[16,128,768]{1,0,2:T(8,128)(2,1)S(1)}, u32[]{:S(2)}) copy-start(bf16[16,128,768]{1,0,2:T(8,128)(2,1)S(1)} %get-tuple-element.145) | copy-start | bytes 9437188
  123.1 9.9 copy-start.1
  151.9 48.4 %copy-start.6 = (f32[1024,768]{0,1:T(8,128)}, f32[1024,768]{0,1:T(8,128)S(1)}, u32[]{:S(2)}) copy-start(f32[1024,768]{0,1:T(8,128)S(1)} %get-tuple-element.159) | copy-start | bytes 9437188
  152.4 8.4 copy-start.30
  152.4 8.4 copy-start.62
  160.8 10.7 %copy-start.18 = (f32[1024,3072]{1,0:T(8,128)}, f32[1024,3072]{1,0:T(8,128)S(1)}, u32[]{:S(2)}) copy-start(f32[1024,3072]{1,0:T(8,128)S(1)} %fusion.143) | copy-start | bytes 37748740
  189.9 10.5 %copy-start.64 = (bf16[1024,3072]{1,0:T(8,128)(2,1)S(1)}, bf16[1024,3072]{1,0:T(8,128)(2,1)}, u32[]{:S(2)}) copy-start(bf16[1024,3072]{1,0:T(8,128)(2,1)} %get-tuple-element.170) | copy-start | bytes 18874372
  233.8 15.0 %slice-start.4 = ((s8[6291456]{0:T(1024)(128)(4,1)}), s8[4194304]{0:T(1024)(128)(4,1)S(1)}, s32[]{:S(2)}) async-start(s8[6291456]{0:T(1024)(128)(4,1)} %bitcast.180), calls=%async_computation.9 | async-start | bytes 8388608
  233.8 19.6 %slice-start.2 = ((s8[6291456]{0:T(1024)(128)(4,1)}), s8[4194304]{0:T(1024)(128)(4,1)S(1)}, s32[]{:S(2)}) async-start(s8[6291456]{0:T(1024)(128)(4,1)} %bitcast.178), calls=%async_computation.7 | async-start | bytes 8388608
  239.6 9.2 slice-start.5
  239.6 9.2 copy-start.2
  239.6 13.8 %slice-start.3 = ((s8[6291456]{0:T(1024)(128)(4,1)}), s8[2097152]{0:T(1024)(128)(4,1)S(1)}, s32[]{:S(2)}) async-start(s8[6291456]{0:T(1024)(128)(4,1)} %bitcast.178), calls=%async_computation.8 | async-start | bytes 4194304
  271.0 9.7 copy-start.36
  324.0 7.3 copy-start.46
  338.0 33.4 %all-to-all-start.2 = ((bf16[8,8,1548]{2,1,0:T(8,128)(2,1)}), bf16[8,8,1548]{2,1,0:T(8,128)(2,1)}, u32[]{:S(2)}, u32[]{:S(2)}) async-start(bf16[8,8,1548]{2,1,0:T(8,128)(2,1)} %pad_maximum_fusion.10), calls=%async_computation.2 | async-start | bytes 425984 | tf_op jit(solution)/shard_map/all_to_all | solution.py:271
  342.0 180.7 %all-reduce.8.cloned.1.call-start = ((), (), s32[]{:S(2)}) async-start(), calls=%async_computation.3 | async-start | bytes 188416 | tf_op jit(solution)/shard_map/psum | solution.py:313
  342.1 23.1 %collective-permute-start.1 = (bf16[64,1548]{1,0:T(8,128)(2,1)}, bf16[64,1548]{1,0:T(8,128)(2,1)}, u32[]{:S(2)}, u32[]{:S(2)}) collective-permute-start(bf16[64,1548]{1,0:T(8,128)(2,1)} %fusion.106), channel_id=1, source_target_pairs={{1,0},{2,1},{3,2},{4,3},{5,4},{6,5},{7,6},{9,8},{10,9},{11,10},{12... | collective-permute-start | bytes 594440 | tf_op jit(solution)/shard_map/ppermute | solution.py:16
  384.9 8.6 copy-start.25
  393.5 571.0 %all-reduce.10.cloned.1.call-start = ((), (), s32[]{:S(2)}) async-start(), calls=%async_computation.4 | async-start | bytes 56623104 | tf_op jit(solution)/shard_map/psum | solution.py:313
  967.1 7.2 copy-start.58
  967.1 7.8 copy-start.43
  967.1 8.4 copy-start.26
  975.5 12.6 %slice-start.6 = ((s8[9437184]{0:T(1024)(128)(4,1)}), s8[4194304]{0:T(1024)(128)(4,1)S(1)}, s32[]{:S(2)}) async-start(s8[9437184]{0:T(1024)(128)(4,1)} %bitcast.190), calls=%async_computation.11 | async-start | bytes 8388608
  978.7 8.8 copy-start.50
  978.7 9.4 slice-start.7
  978.7 9.4 slice-start.8
  (49 other events, 185.1 us)
Sparse Core Ops, SparseCore 0:
  393.6 129.0 all-reduce.7
  531.4 433.1 all-reduce.9
where the time goes:
time: 1010 us; the launch traced here: 999 us
  waiting for transfers between devices  540 us (53%)
  matrix products  169 us (17%)
  local copies, waits for them, and re-layouts  161 us (16%)
  other arithmetic  96.7 us (10%)
  starting transfers between devices  17.9 us (2%)
  between operations  15 us (1%)
    psum x2, waiting for transfers between devices, per_device(): lax.psum((first_gain_grad, first_shift_grad, joint_weight_grad, query_bia...  537 us
    unnamed x167, local copies, waits for them, and re-layouts  50.3 us
    dot_general x5, matrix products, times_transposed(): lax.dot_general(left, right, (((1,), (1,)), ((), ())), preferred_element_...  38.9 us
    dot_general x5, matrix products, cross(): lax.dot_general(left, right, (((0,), (0,)), ((), ())), preferred_element_...  32.2 us
  transfers between devices with their start and end apart: 7, of which 3 were waited for; matrix products, arithmetic and copies ran while one was open for 13% of the time, Pallas kernels for 0%

commit v1 on v0

--- a/solution.py
+++ b/solution.py
@@ -295,6 +295,11 @@
     out_weight_grad = cross(mixed_low, grad_attn_low)
     expand_weight_grad = cross(normed_two_low, grad_pre_low)
     reduce_weight_grad = cross(hidden_low, grad_out_low)
+
+    def form_sections(block_in):
+        a_next = jax.lax.psum(jax.lax.psum(block_in, "seq"), "dp")
+        return a_next
+
     (
         first_gain_grad,
         first_shift_grad,
@@ -310,7 +315,7 @@
         expand_bias_grad,
         reduce_weight_grad,
         reduce_bias_grad,
-    ) = lax.psum(
+    ) = form_sections(
         (
             first_gain_grad,
             first_shift_grad,
@@ -326,8 +331,7 @@
             expand_bias_grad,
             reduce_weight_grad,
             reduce_bias_grad,
-        ),
-        ("dp", "seq"),
+        )
     )
     return (
         layer_out[None],

time: 1010 us -> 1830 us (1.81)
  waiting for transfers between devices: 540 us -> 1360 us
    psum x2 -> x4, waiting for transfers between devices: 537 us -> 1350 us  [form_sections(): a_next = jax.lax.psum(jax.lax.psum(block_in, 'seq'), 'dp')]
  transfers between devices with their start and end apart: 7 -> 9, of which waited for: 3 -> 5; matrix products, arithmetic and copies ran while one was open for 13% -> 7% of each run, Pallas kernels for 0% -> 0%
where the time goes in v1:
time: 1830 us; the launch traced here: 1820 us
  waiting for transfers between devices  1360 us (74%)
  matrix products  169 us (9%)
  local copies, waits for them, and re-layouts  161 us (9%)
  other arithmetic  96.6 us (5%)
    psum x4, waiting for transfers between devices, form_sections(): a_next = jax.lax.psum(jax.lax.psum(block_in, 'seq'), 'dp')  1350 us
    unnamed x167, local copies, waits for them, and re-layouts  50.3 us
    dot_general x5, matrix products, times_transposed(): lax.dot_general(left, right, (((1,), (1,)), ((), ())), preferred_element_...  38.9 us
  transfers between devices with their start and end apart: 9, of which 5 were waited for; matrix products, arithmetic and copies ran while one was open for 7% of the time, Pallas kernels for 0%

profile of v1, /device:TPU:0, one launch (start us, length us, event | category | flops | bytes accessed | tf_op | source)
XLA Modules:
  0.0 1815.5 jit_solution(13978368618682900913)
XLA Ops:
  58.0 9.3 copy.263
  83.4 7.7 fusion.147
  98.4 9.3 copy.262
  116.1 6.9 fusion.148
  152.3 8.4 fusion.143
  160.7 10.7 fusion.73
  171.4 18.3 %convert_reduce_fusion = (f32[3072]{0:T(1024)}, bf16[1024,3072]{1,0:T(8,128)(2,1)}) fusion(bf16[3072,768]{1,0:T(8,128)(2,1)} %param.32, bf16[1,1024,768]{2,1,0:T(8,128)(2,1)} %param.19, f32[1024,3072]{1,0:T(8,128)S(1)} %fusion.143, f32[3072]{0:T(1024)S(1)} %copy-done.62), kind=kOutput, calls=%fused_computation.13 | convolution fusion | flops 4916769792 | bytes 25190400 | tf_op jit(solution)/shard_map/dot_general | solution.py:51
  189.7 10.5 fusion.150
  200.2 7.9 fusion.142
  233.6 5.8 fusion.94
  239.4 9.2 multiply_reduce_fusion
  264.3 6.6 copy.298
  270.8 9.7 multiply_convert_fusion.2
  283.5 7.4 fusion.54
  290.9 6.5 copy.297
  297.4 9.9 pad_maximum_fusion
  307.3 11.5 fusion.144
  343.2 8.6 convert_reduce_fusion.1
  352.4 6.5 copy.330
  359.0 6.1 reshape.331
  365.0 6.2 bitcast_add_fusion
  371.2 7.4 scatter_custom_fusion
  386.4 6.9 fusion.28
  393.4 9.6 fusion.38
  403.1 48.0 %all-reduce.12.cloned.1.call-done = (f32[768]{0:T(1024)}, f32[768]{0:T(1024)}, f32[768]{0:T(1024)}, f32[768]{0:T(1024)}, f32[768,12]{0,1:T(8,128)}, /*index=5*/f...) async-done(((f32[768]{0:T(1024)}, f32[768]{0:T(1024)}, f32[768]{0:T(1024)}, f32[768]{0:T(1024)}, f32[768,12]{0,1:T(8,128)}, ...) | async-done | bytes 73744 | tf_op jit(solution)/shard_map/psum | solution.py:300
  451.2 349.7 %all-reduce.14.cloned.1.call-done = (f32[768,2304]{1,0:T(8,128)}, f32[768,768]{1,0:T(8,128)}, f32[768,3072]{1,0:T(8,128)}, f32[3072,768]{1,0:T(8,128)}) async-done(((f32[768,2304]{1,0:T(8,128)}, f32[768,768]{1,0:T(8,128)}, f32[768,3072]{1,0:T(8,128)}, f32[3072,768]{1,0:T(8,128)}), (f32[768,2304]{1,0:T(8,128)}, f32[768,768]{1,0:T(8,128)}, f32[768,3072]{1,0:T(8,128)}, ...) | async-done | bytes 28311568 | tf_op jit(solution)/shard_map/psum | solution.py:300
  800.9 11.9 fusion.78
  816.1 6.0 fusion.27
  825.6 14.4 all-reduce.16.cloned.1.call-done
  840.0 940.9 %all-reduce.18.cloned.1.call-done = (f32[768,2304]{1,0:T(8,128)}, f32[768,768]{1,0:T(8,128)}, f32[768,3072]{1,0:T(8,128)}, f32[3072,768]{1,0:T(8,128)}) async-done(((f32[768,2304]{1,0:T(8,128)}, f32[768,768]{1,0:T(8,128)}, f32[768,3072]{1,0:T(8,128)}, f32[3072,768]{1,0:T(8,128)}), (f32[768,2304]{1,0:T(8,128)}, f32[768,768]{1,0:T(8,128)}, f32[768,3072]{1,0:T(8,128)}, ...) | async-done | bytes 28311568 | tf_op jit(solution)/shard_map/psum | solution.py:300
  1783.4 6.6 copy.445
  1795.0 8.8 copy.453
  (273 shorter events, 207.8 us)
Async XLA Ops:
  7.2 17.4 copy-start
  7.2 13.0 copy-start.47
  7.2 13.0 copy-start.51
  8.7 58.5 %all-to-all-start = ((s32[8,1,8]{2,1,0:T(1,128)}), s32[8,1,8]{2,1,0:T(1,128)}, u32[]{:S(2)}, u32[]{:S(2)}) async-start(s32[8,1,8]{2,1,0:T(1,128)} %bitcast.8), calls=%async_computation | async-start | bytes 8192 | tf_op jit(solution)/shard_map/all_to_all | solution.py:209
  35.6 57.2 %collective-permute-start = (bf16[64,1548]{1,0:T(8,128)(2,1)}, bf16[64,1548]{1,0:T(8,128)(2,1)}, u32[]{:S(2)}, u32[]{:S(2)}) collective-permute-start(bf16[64,1548]{1,0:T(8,128)(2,1)} %slice.111), channel_id=1, source_target_pairs={{0,1},{1,2},{2,3},{3,4},{4,5},{5,6},{6,7},{8,9},{9,10},{10,11},{11... | collective-permute-start | bytes 594440 | tf_op jit(solution)/shard_map/ppermute | solution.py:16
  67.3 10.6 all-to-all-start.1
  116.0 16.9 copy-start.10
  123.0 9.9 copy-start.1
  151.8 48.4 %copy-start.6 = (f32[1024,768]{0,1:T(8,128)}, f32[1024,768]{0,1:T(8,128)S(1)}, u32[]{:S(2)}) copy-start(f32[1024,768]{0,1:T(8,128)S(1)} %get-tuple-element.173) | copy-start | bytes 9437188
  152.3 8.4 copy-start.30
  152.3 8.4 copy-start.62
  160.7 10.7 copy-start.18
  189.7 10.5 copy-start.64
  233.6 15.0 slice-start.4
  233.6 19.4 %slice-start.2 = ((s8[6291456]{0:T(1024)(128)(4,1)}), s8[4194304]{0:T(1024)(128)(4,1)S(1)}, s32[]{:S(2)}) async-start(s8[6291456]{0:T(1024)(128)(4,1)} %bitcast.178), calls=%async_computation.9 | async-start | bytes 8388608
  239.4 9.2 slice-start.5
  239.4 9.2 copy-start.2
  239.4 13.6 slice-start.3
  270.8 9.7 copy-start.36
  337.8 33.4 %all-to-all-start.2 = ((bf16[8,8,1548]{2,1,0:T(8,128)(2,1)}), bf16[8,8,1548]{2,1,0:T(8,128)(2,1)}, u32[]{:S(2)}, u32[]{:S(2)}) async-start(bf16[8,8,1548]{2,1,0:T(8,128)(2,1)} %pad_maximum_fusion.10), calls=%async_computation.2 | async-start | bytes 425984 | tf_op jit(solution)/shard_map/all_to_all | solution.py:271
  341.8 109.3 %all-reduce.12.cloned.1.call-start = ((), (), s32[]{:S(2)}) async-start(), calls=%async_computation.3 | async-start | bytes 188416 | tf_op jit(solution)/shard_map/psum | solution.py:300
  341.9 23.1 %collective-permute-start.1 = (bf16[64,1548]{1,0:T(8,128)(2,1)}, bf16[64,1548]{1,0:T(8,128)(2,1)}, u32[]{:S(2)}, u32[]{:S(2)}) collective-permute-start(bf16[64,1548]{1,0:T(8,128)(2,1)} %fusion.106), channel_id=1, source_target_pairs={{1,0},{2,1},{3,2},{4,3},{5,4},{6,5},{7,6},{9,8},{10,9},{11,10},{12... | collective-permute-start | bytes 594440 | tf_op jit(solution)/shard_map/ppermute | solution.py:16
  384.7 8.6 copy-start.25
  393.4 407.5 %all-reduce.14.cloned.1.call-start = ((), (), s32[]{:S(2)}) async-start(), calls=%async_computation.4 | async-start | bytes 56623104 | tf_op jit(solution)/shard_map/psum | solution.py:300
  403.1 437.0 %all-reduce.16.cloned.1.call-start = ((), (), s32[]{:S(2)}) async-start(), calls=%async_computation.5 | async-start | bytes 188416 | tf_op jit(solution)/shard_map/psum | solution.py:300
  451.2 1329.7 %all-reduce.18.cloned.1.call-start = ((), (), s32[]{:S(2)}) async-start(), calls=%async_computation.6 | async-start | bytes 56623104 | tf_op jit(solution)/shard_map/psum | solution.py:300
  1783.4 7.8 copy-start.43
  1783.4 8.4 copy-start.26
  1791.8 12.6 slice-start.6
  1795.0 8.8 copy-start.50
  1795.0 9.4 slice-start.7
  1795.0 9.4 slice-start.8
  (51 other events, 199.2 us)
Sparse Core Ops, SparseCore 0:
  393.5 57.6 all-reduce.11
  457.2 343.6 all-reduce.13
  804.4 35.5 all-reduce.15
  842.8 938.0 all-reduce.17
